TPU v7x, 32 devices: a whole 2x2x4 slice. The times are simulated.
32 devices in a mesh: parts: 2 (over y), hidden: 16 (over z, x, core).
Axes of the slice: x: 2, y: 2, z: 4, core: 2. Of those that a mesh axis runs over, the one named last changes fastest.
Arguments:
- tokens: bfloat16 [2, 128, 3072], P(None, ('parts', 'hidden')), parts along dimension 1, may hold values from -6 to 6
- route_ids: int32 [2, 128, 2], P(None, ('parts', 'hidden')), parts along dimension 1, may hold values from 0 to 7, all different within a row; in each aligned block of 4 rows (0 to 3, 4 to 7, ..., all dimensions but the last counted through in order) at most 2 rows name the same one
- route_weight: float32 [2, 128, 2], P(None, ('parts', 'hidden')), parts along dimension 1, may hold values from 0.1 to 0.9
- gate_weight: bfloat16 [3072, 65536], P(None, 'hidden'), may hold values from -0.109375 to 0.109375
- up_weight: bfloat16 [3072, 65536], P(None, 'hidden'), may hold values from -0.109375 to 0.109375
- down_weight: bfloat16 [65536, 3072], P('hidden'), may hold values from -0.0625 to 0.0625
Outputs:
- mixed: bfloat16 [2, 128, 3072], P(None, ('parts', 'hidden')), parts along dimension 1
There are 2 independent parts, one for each index of `parts`. A program takes and returns all parts, laid end to end along the dimension named above; an argument that names none is the same for every part. Nothing has to cross between parts.
Inputs may be any that keep to these rules, and one draw needn't show every extreme that they name: `route_ids`: each row names 2 different experts. Among the rows of one device in one step (aligned blocks of 4 rows), at most 2 name the same expert, and in every draw some expert is named by exactly 2 of them.
All inputs are finite; a program needn't handle non-finite values.
Results may differ from a plain program's by a relative error of at most 0.009.
Values may be sent and summed in bfloat16 or wider, within the bound.
A program may use at most 192 MiB of HBM per device.

v0:
```python
import jax
import jax.numpy as jnp
from jax import lax
from jax.sharding import PartitionSpec as P

EXPERTS = 8
MOST = 2


def routing_tables(route_rows, weight_rows, places_count):
    experts = jnp.arange(EXPERTS, dtype=jnp.int32)
    matches = route_rows[None, :, :] == experts[:, None, None]
    picked = jnp.any(matches, axis=2).astype(jnp.int32)
    before = jnp.cumsum(picked, axis=1) - picked
    places = jnp.arange(places_count, dtype=jnp.int32)
    chooser = ((before[:, None, :] == places[None, :, None]) & (picked[:, None, :] == 1)).astype(
        jnp.float32
    )
    shares = jnp.sum(jnp.where(matches, weight_rows[None, :, :], 0.0), axis=2)
    factors = jnp.where(picked == 1, shares, 0.0)
    slot_of = jnp.minimum(before, places_count - 1)
    return (chooser, (slot_of, factors))


def pack_rows(chooser, token_rows, group):
    packed = jnp.einsum(
        "esr,rd->esd", chooser.astype(jnp.bfloat16), token_rows, preferred_element_type=jnp.float32
    )
    return jnp.repeat(packed.astype(jnp.bfloat16), group, axis=0)


def expert_apply(received, gate_weight, up_weight, down_weight):
    width = received.shape[-1]
    flat = received.reshape(-1, width)
    gate = jnp.dot(flat, gate_weight, preferred_element_type=jnp.float32)
    upward = jnp.dot(flat, up_weight, preferred_element_type=jnp.float32)
    hidden = (jax.nn.silu(gate) * upward).astype(jnp.bfloat16)
    partial_value = jnp.dot(hidden, down_weight, preferred_element_type=jnp.float32).astype(
        jnp.bfloat16
    )
    return partial_value.reshape(received.shape)


def combine(returned, lookup, group):
    slot_of, factors = lookup
    devices, places_count, width = returned.shape
    summed = jnp.sum(
        returned.reshape(EXPERTS, group, places_count, width).astype(jnp.float32), axis=1
    )
    fetched = jnp.take_along_axis(summed, slot_of[:, :, None], axis=1)
    return jnp.sum(factors[:, :, None] * fetched, axis=0)


def on_device(tokens, route_ids, route_weight, gate_weight, up_weight, down_weight):
    devices = lax.axis_size("hidden")
    group = devices // EXPERTS
    steps_count = tokens.shape[0]
    tables = [
        routing_tables(route_ids[step_index], route_weight[step_index], MOST)
        for step_index in range(steps_count)
    ]
    results = []
    packed = jnp.concatenate(
        [
            pack_rows(tables[step_index][0], tokens[step_index], group)
            for step_index in range(steps_count)
        ],
        axis=1,
    )
    returned = lax.all_to_all(
        expert_apply(
            lax.all_to_all(packed, "hidden", split_axis=0, concat_axis=0, tiled=True),
            gate_weight,
            up_weight,
            down_weight,
        ),
        "hidden",
        split_axis=0,
        concat_axis=0,
        tiled=True,
    )
    for step_index in range(steps_count):
        part_back = returned[:, step_index * MOST : (step_index + 1) * MOST]
        results.append(combine(part_back, tables[step_index][1], group))
    return jnp.stack(results, axis=0).astype(jnp.bfloat16)


def solution(mesh):
    placed = (
        P(None, ("parts", "hidden"), None),
        P(None, ("parts", "hidden"), None),
        P(None, ("parts", "hidden"), None),
        P(None, "hidden"),
        P(None, "hidden"),
        P("hidden", None),
    )
    return jax.shard_map(
        on_device,
        mesh=mesh,
        in_specs=placed,
        out_specs=P(None, ("parts", "hidden"), None),
        check_vma=False,
    )
```

profile of v0, /device:TPU:0, one launch (start us, length us, event | category | flops | bytes accessed | tf_op | source)
XLA Modules:
  0.0 75.2 jit_solution(1696346059147473080)
XLA Ops:
  0.0 0.7 slice_bitcast_fusion.3
  0.8 1.0 %convolution_convert_fusion.2 = bf16[8,2,3072]{2,0,1:T(8,128)(2,1)S(1)} fusion(bf16[2,4,3072]{2,1,0:T(4,128)(2,1)} %param.8, s32[8,4]{0,1:T(4,128)S(1)} %get-tuple-element.9, pred[8,4]{0,1:T(4,128)(4,1)S(1)} %get-tuple-element.16), kind=kOutput, calls=%fused_computation.6 | convolution fusion | flops 442624 | bytes 123040 | tf_op jit(solution)/shard_map/esr,rd->esd/dot_general | solution.py:26
  1.8 0.1 copy.33
  2.0 1.0 %convolution_convert_fusion.1 = bf16[8,2,3072]{2,0,1:T(8,128)(2,1)S(1)} fusion(bf16[2,4,3072]{2,1,0:T(4,128)(2,1)} %param.8, s32[8,4]{0,1:T(4,128)S(1)} %get-tuple-element.11, pred[8,4]{0,1:T(4,128)(4,1)S(1)} %get-tuple-element.18), kind=kOutput, calls=%fused_computation.5 | convolution fusion | flops 442624 | bytes 123040 | tf_op jit(solution)/shard_map/esr,rd->esd/dot_general | solution.py:26
  2.9 0.1 copy.34
  3.0 0.1 broadcast_in_dim.55
  3.2 0.1 broadcast_in_dim.56
  3.3 1.1 %pad_maximum_fusion = bf16[16,4,3072]{2,1,0:T(4,128)(2,1)} fusion(bf16[16,2,3072]{2,1,0:T(2,128)(2,1)S(1)} %bitcast.56, bf16[16,2,3072]{2,1,0:T(2,128)(2,1)S(1)} %bitcast.55), kind=kLoop, calls=%fused_computation.13 | loop fusion | flops 786432 | bytes 786432 | tf_op jit(solution)/shard_map/concatenate | solution.py:63
  4.4 7.4 %all-to-all-start = ((bf16[16,4,3072]{2,1,0:T(4,128)(2,1)}), bf16[16,4,3072]{2,1,0:T(4,128)(2,1)S(1)}, u32[]{:S(2)}, u32[]{:S(2)}) async-start(bf16[16,4,3072]{2,1,0:T(4,128)(2,1)} %pad_maximum_fusion), calls=%async_computation | async-start | bytes 786432 | tf_op jit(solution)/shard_map/all_to_all | solution.py:72
  12.1 0.7 slice_bitcast_fusion.2
  12.8 11.2 %all-to-all-done = bf16[16,4,3072]{2,1,0:T(4,128)(2,1)S(1)} async-done(((bf16[16,4,3072]{2,1,0:T(4,128)(2,1)}), bf16[16,4,3072]{2,1,0:T(4,128)(2,1)S(1)}, u32[]{:S(2)}, u32[]{:S(2)}) %all-to-all-start) | async-done | bytes 393248 | tf_op jit(solution)/shard_map/all_to_all | solution.py:72
  24.1 10.5 %fusion.22 = f32[64,4096]{1,0:T(8,128)S(1)} fusion(bf16[64,3072]{1,0:T(8,128)(2,1)S(1)} %reshape.95, bf16[3072,4096]{1,0:T(8,128)(2,1)} %param.11), kind=kOutput, calls=%fused_computation.61 | convolution fusion | flops 1610612736 | bytes 26607616 | tf_op jit(solution)/shard_map/dot_general | solution.py:35
  34.6 19.9 %convolution_convert_fusion = bf16[64,3072]{1,0:T(8,128)(2,1)S(1)} fusion(bf16[4096,3072]{1,0:T(8,128)(2,1)} %param.13, bf16[64,3072]{1,0:T(8,128)(2,1)S(1)} %reshape.95, bf16[3072,4096]{1,0:T(8,128)(2,1)} %param.12, f32[64,4096]{1,0:T(8,128)S(1)} %fusion.22), kind=kOutput, calls=%fused_computation.4 | convolution fusion | flops 3222994944 | bytes 52166656 | tf_op jit(solution)/shard_map/dot_general | solution.py:38
  54.4 0.9 %reshape.96 = bf16[16,4,3072]{2,1,0:T(4,128)(2,1)} reshape(bf16[64,3072]{1,0:T(8,128)(2,1)S(1)} %convolution_convert_fusion) | data formatting | bytes 786432 | tf_op jit(solution)/shard_map/reshape | solution.py:41
  55.3 3.6 %all-to-all-start.1 = ((bf16[16,4,3072]{2,1,0:T(4,128)(2,1)}), bf16[16,4,3072]{2,1,0:T(4,128)(2,1)S(1)}, u32[]{:S(2)}, u32[]{:S(2)}) async-start(bf16[16,4,3072]{2,1,0:T(4,128)(2,1)} %reshape.96), calls=%async_computation.1 | async-start | bytes 786432 | tf_op jit(solution)/shard_map/all_to_all | solution.py:70
  59.4 11.6 %all-to-all-done.1 = bf16[16,4,3072]{2,1,0:T(4,128)(2,1)S(1)} async-done(((bf16[16,4,3072]{2,1,0:T(4,128)(2,1)}), bf16[16,4,3072]{2,1,0:T(4,128)(2,1)S(1)}, u32[]{:S(2)}, u32[]{:S(2)}) %all-to-all-start.1) | async-done | bytes 393248 | tf_op jit(solution)/shard_map/all_to_all | solution.py:70
  71.1 0.5 convert_reduce_fusion.1
  71.6 1.2 %gather_fusion = f32[32,3072]{1,0:T(8,128)S(1)} fusion(f32[8,2,3072]{2,1,0:T(2,128)S(1)} %get-tuple-element.6, s32[32]{0:T(128)S(1)} %reshape.111), kind=kCustom, calls=%fused_computation.clone | custom fusion | bytes 786688 | tf_op jit(solution)/shard_map/jit(take_along_axis)/gather | solution.py:50
  72.7 0.1 reshape.114
  72.9 1.2 %gather_fusion.1 = f32[32,3072]{1,0:T(8,128)S(1)} fusion(f32[8,2,3072]{2,1,0:T(2,128)S(1)} %get-tuple-element.7, s32[32]{0:T(128)S(1)} %reshape.115), kind=kCustom, calls=%fused_computation.1.clone | custom fusion | bytes 786688 | tf_op jit(solution)/shard_map/jit(take_along_axis)/gather | solution.py:50
  74.0 0.1 reshape.118
  74.1 0.2 fusion.8
  74.3 0.2 fusion.7
  74.5 0.7 pad_maximum_fusion.1
  (21 shorter events, 1.1 us)
Async XLA Ops:
  4.4 19.6 %all-to-all-start = ((bf16[16,4,3072]{2,1,0:T(4,128)(2,1)}), bf16[16,4,3072]{2,1,0:T(4,128)(2,1)S(1)}, u32[]{:S(2)}, u32[]{:S(2)}) async-start(bf16[16,4,3072]{2,1,0:T(4,128)(2,1)} %pad_maximum_fusion), calls=%async_computation | async-start | bytes 786432 | tf_op jit(solution)/shard_map/all_to_all | solution.py:72
  55.3 15.7 %all-to-all-start.1 = ((bf16[16,4,3072]{2,1,0:T(4,128)(2,1)}), bf16[16,4,3072]{2,1,0:T(4,128)(2,1)S(1)}, u32[]{:S(2)}, u32[]{:S(2)}) async-start(bf16[16,4,3072]{2,1,0:T(4,128)(2,1)} %reshape.96), calls=%async_computation.1 | async-start | bytes 786432 | tf_op jit(solution)/shard_map/all_to_all | solution.py:70
where the time goes:
time: 75.6 us; the launch traced here: 75.2 us
  matrix products  32.3 us (43%)
  waiting for transfers between devices  22.8 us (30%)
  starting transfers between devices  10.9 us (14%)
  local copies, waits for them, and re-layouts  6.04 us (8%)
  other arithmetic  2.98 us (4%)
    dot_general x1, matrix products, expert_apply(): jnp.dot(hidden, down_weight, preferred_element_type=jnp.float32)  19.9 us
    all_to_all x1, waiting for transfers between devices, on_device(): lax.all_to_all(expert_apply(lax.all_to_all(packed, 'hidden', split_axis=0...  11.6 us
    all_to_all x1, waiting for transfers between devices, on_device(): lax.all_to_all(packed, 'hidden', split_axis=0, concat_axis=0, tiled=True)  11.2 us
    dot_general x1, matrix products, expert_apply(): gate = jnp.dot(flat, gate_weight, preferred_element_type=jnp.float32)  10.5 us
    all_to_all x1, starting transfers between devices, on_device(): lax.all_to_all(packed, 'hidden', split_axis=0, concat_axis=0, tiled=True)  7.36 us
    all_to_all x1, starting transfers between devices, on_device(): lax.all_to_all(expert_apply(lax.all_to_all(packed, 'hidden', split_axis=0...  3.55 us
    gather x8, local copies, waits for them, and re-layouts, combine(): fetched = jnp.take_along_axis(summed, slot_of[:, :, None], axis=1)  2.89 us
    dot_general x2, matrix products, pack_rows(): jnp.einsum('esr,rd->esd', chooser.astype(jnp.bfloat16), token_rows, prefe...  1.9 us
  transfers between devices with their start and end apart: 2, of which 2 were waited for; matrix products, arithmetic and copies ran while one was open for 2% of the time, Pallas kernels for 0%

commit v1 on v0

v1 whole, which is shorter than its diff:
```python
import functools

import jax
import jax.numpy as jnp
from jax import lax
from jax.experimental import pallas as pl
from jax.experimental.pallas import tpu as pltpu
from jax.sharding import PartitionSpec as P

EXPERTS = 8
MOST = 2
UNIT = 1024
WIDE = 512
SLOTS = 56
MESH = pl.DeviceIdType.MESH


def routing(ids, shares, steps, rows, experts, step_of, slot_of, row, owner_axis):
    shape = experts.shape
    before = jnp.zeros(shape, jnp.int32)
    picked = jnp.zeros(shape, jnp.int32)
    factor = jnp.zeros(shape, jnp.float32)
    for number in range(steps * rows):
        step, place = number // rows, number % rows
        first, second = ids[step, place, 0], ids[step, place, 1]
        named_first, named_second = experts == first, experts == second
        named = jnp.where(named_first | named_second, 1, 0)
        share = jnp.where(named_first, shares[step, place, 0], 0.0) + jnp.where(
            named_second, shares[step, place, 1], 0.0
        )
        here = row == number
        picked = jnp.where(here, named, picked)
        factor = jnp.where(here, share, factor)
        later = (row > number) & (row < (step + 1) * rows)
        before = before + jnp.where(later, named, 0)
    chosen = (picked == 1) & (before == slot_of) & (row // rows == step_of)
    return jnp.where(chosen, 1.0, 0.0), jnp.where(chosen, factor, 0.0)


def kernel(
    n,
    tokens,
    ids,
    shares,
    gate,
    up,
    down,
    out,
    send,
    near,
    far,
    staged,
    x,
    w,
    hidden,
    kept,
    give,
    take,
    sums,
    back,
    factors,
    w_sem,
    send_sem,
    near_sem,
    pass_sem,
    far_sem,
    give_sem,
    take_sem,
    sums_sem,
    back_sem,
    own_sem,
):
    steps, rows, width = tokens.shape
    units = gate.shape[1]
    chips = n // 2
    places = steps * MOST
    per_expert = chips // EXPERTS
    me = lax.axis_index("hidden")
    core, chip = lax.rem(me, 2), me // 2
    sibling = {"hidden": chip * 2 + (1 - core)}
    slots = w.shape[0]
    deep = width // UNIT
    blocks_up = units // WIDE
    first_units = 2 * deep * blocks_up
    down_rows = min(UNIT, units)
    down_deep = units // down_rows
    blocks_down = width // WIDE
    down_units = down_deep * blocks_down
    early = min(down_units, slots - first_units)

    def peer(distance):
        return lax.rem(chip + distance, chips)

    def device(other):
        return {"hidden": other * 2 + core}

    def up_copy(block, i, ref, base):
        slot = block * 2 * deep + base + i
        return pltpu.make_async_copy(
            ref.at[pl.ds(i * UNIT, UNIT), pl.ds(pl.multiple_of(block * WIDE, WIDE), WIDE)],
            w.at[slot],
            w_sem.at[slot],
        )

    def up_copies(block):
        return [up_copy(block, i, gate, 0) for i in range(deep)] + [
            up_copy(block, i, up, deep) for i in range(deep)
        ]

    def down_copy(number):
        block, i = number // down_deep, lax.rem(number, down_deep)
        slot = lax.rem(first_units + number, slots)
        return pltpu.make_async_copy(
            down.at[
                pl.ds(pl.multiple_of(i * down_rows, down_rows), down_rows),
                pl.ds(pl.multiple_of(block * WIDE, WIDE), WIDE),
            ],
            w.at[slot, pl.ds(0, down_rows), :],
            w_sem.at[slot],
        )

    barrier = pltpu.get_barrier_semaphore()

    def greet(distance, carry):
        pl.semaphore_signal(barrier, inc=1, device_id=device(peer(distance)), device_id_type=MESH)
        return carry

    lax.fori_loop(1, chips, greet, 0)
    pl.semaphore_signal(barrier, inc=1, device_id=sibling, device_id_type=MESH)

    def start_up(block, carry):
        for copy in up_copies(block):
            copy.start()
        return carry

    lax.fori_loop(0, blocks_up, start_up, 0)

    many = EXPERTS * places
    place = lax.broadcasted_iota(jnp.int32, (many, steps * rows), 0)
    row = lax.broadcasted_iota(jnp.int32, (many, steps * rows), 1)
    chooser, _ = routing(
        ids, shares, steps, rows, place // places, place % places // MOST, place % MOST, row, 1
    )
    owned = jnp.concatenate([tokens[step].astype(jnp.float32) for step in range(steps)], axis=0)
    packed = jnp.dot(chooser, owned, preferred_element_type=jnp.float32)
    for expert in range(EXPERTS):
        send[expert] = packed[expert * places : (expert + 1) * places].astype(jnp.bfloat16)

    pl.semaphore_wait(barrier, chips)

    def send_copy(distance):
        other = peer(distance)
        return pltpu.make_async_remote_copy(
            src_ref=send.at[other // per_expert],
            dst_ref=near.at[chip],
            send_sem=send_sem.at[other],
            recv_sem=near_sem.at[chip],
            device_id=device(other),
            device_id_type=MESH,
        )

    def arrival(source):
        return pltpu.make_async_remote_copy(
            src_ref=send.at[0],
            dst_ref=near.at[source],
            send_sem=send_sem.at[source],
            recv_sem=near_sem.at[source],
            device_id=device(source),
            device_id_type=MESH,
        )

    def pass_copy(source):
        return pltpu.make_async_remote_copy(
            src_ref=near.at[source],
            dst_ref=far.at[source],
            send_sem=pass_sem.at[source],
            recv_sem=far_sem.at[source],
            device_id=sibling,
            device_id_type=MESH,
        )

    def start_send(distance, carry):
        send_copy(distance).start()
        return carry

    lax.fori_loop(1, chips, start_send, 0)
    own = pltpu.make_async_copy(send.at[chip // per_expert], near.at[chip], own_sem)
    own.start()

    def start_down(number, carry):
        down_copy(number).start()
        return carry

    lax.fori_loop(0, early, start_down, 0)

    own.wait()
    pass_copy(chip).start()

    def forward(distance, carry):
        source = lax.rem(chip - distance + chips, chips)
        arrival(source).wait_recv()
        pass_copy(source).start()
        return carry

    lax.fori_loop(1, chips, forward, 0)

    count = chips * places
    row = lax.broadcasted_iota(jnp.int32, (steps * rows, count), 0)
    place = lax.broadcasted_iota(jnp.int32, (steps * rows, count), 1)
    _, found = routing(
        ids,
        shares,
        steps,
        rows,
        place // (places * per_expert),
        place % places // MOST,
        place % MOST,
        row,
        0,
    )
    factors[...] = found

    pairs = 8 // places

    def stage_near(group, carry):
        staged[group] = jnp.concatenate(
            [near[group * pairs + i].astype(jnp.float32) for i in range(pairs)], axis=0
        )
        return carry

    lax.fori_loop(0, chips // pairs, stage_near, 0)

    def await_far(source, carry):
        pass_copy(source).wait()
        return carry

    lax.fori_loop(0, chips, await_far, 0)

    def stage_far(group, carry):
        staged[chips // pairs + group] = jnp.concatenate(
            [far[group * pairs + i].astype(jnp.float32) for i in range(pairs)], axis=0
        )
        return carry

    lax.fori_loop(0, chips // pairs, stage_far, 0)
    x[...] = staged[...].reshape(x.shape).astype(jnp.bfloat16)

    def up_block(block, carry):
        copies = up_copies(block)
        base = block * 2 * deep
        for copy in copies[:deep]:
            copy.wait()
        gated = jnp.dot(
            x[...],
            w[pl.ds(base, deep)].reshape(width, WIDE),
            preferred_element_type=jnp.float32,
        )
        for copy in copies[deep:]:
            copy.wait()
        upward = jnp.dot(
            x[...],
            w[pl.ds(base + deep, deep)].reshape(width, WIDE),
            preferred_element_type=jnp.float32,
        )
        value = gated / (1.0 + jnp.exp(-gated)) * upward
        hidden[:, pl.ds(pl.multiple_of(block * WIDE, WIDE), WIDE)] = value.astype(jnp.bfloat16)
        for i in range(2 * deep):
            number = early + block * 2 * deep + i

            @pl.when(number < down_units)
            def _():
                down_copy(number).start()

        return carry

    lax.fori_loop(0, blocks_up, up_block, 0)

    half = chips * places

    def give_copy(block):
        return pltpu.make_async_remote_copy(
            src_ref=give.at[block],
            dst_ref=take.at[block],
            send_sem=give_sem.at[block],
            recv_sem=take_sem.at[block],
            device_id=sibling,
            device_id_type=MESH,
        )

    def back_copy(block, distance):
        other = peer(distance)
        return pltpu.make_async_remote_copy(
            src_ref=sums.at[block, other],
            dst_ref=back.at[block, chip],
            send_sem=sums_sem.at[block, other],
            recv_sem=back_sem.at[block, chip],
            device_id=device(other),
            device_id_type=MESH,
        )

    def back_arrival(block, source):
        return pltpu.make_async_remote_copy(
            src_ref=sums.at[block, source],
            dst_ref=back.at[block, source],
            send_sem=sums_sem.at[block, source],
            recv_sem=back_sem.at[block, source],
            device_id=device(source),
            device_id_type=MESH,
        )

    def compute(block):
        for i in range(down_deep):
            down_copy(block * down_deep + i).wait()
        slot = lax.rem(first_units + block * down_deep, slots)
        weights = w[pl.ds(slot, down_deep), pl.ds(0, down_rows), :].reshape(units, WIDE)
        partial = jnp.dot(hidden[...], weights, preferred_element_type=jnp.float32)
        kept[block] = partial[:half]
        give[block] = partial[half:].astype(jnp.bfloat16)
        give_copy(block).start()

    def exchange(block):
        give_copy(block).wait_recv()
        total = kept[block] + take[block].astype(jnp.float32)
        for other in range(chips):
            sums[block, other] = total[other * places : (other + 1) * places].astype(jnp.bfloat16)

        def start_back(distance, carry):
            back_copy(block, distance).start()
            return carry

        lax.fori_loop(1, chips, start_back, 0)
        back[block, chip] = sums[block, chip]

    def combine(block):
        def await_back(distance, carry):
            back_arrival(block, lax.rem(chip - distance + chips, chips)).wait_recv()
            return carry

        lax.fori_loop(1, chips, await_back, 0)
        pieces = jnp.concatenate(
            [back[block, source].astype(jnp.float32) for source in range(chips)], axis=0
        )
        mixed = jnp.dot(
            factors[...],
            pieces,
            preferred_element_type=jnp.float32,
            precision=lax.Precision.HIGHEST,
        )
        columns = pl.ds(pl.multiple_of(block * WIDE, WIDE), WIDE)
        for step in range(steps):
            out[step, :, columns] = mixed[step * rows : (step + 1) * rows]

    lag = 3

    def down_block(block, carry):
        compute(block)

        @pl.when(block >= 1)
        def _():
            exchange(block - 1)

        @pl.when(block >= lag)
        def _():
            combine(block - lag)

        return carry

    lax.fori_loop(0, blocks_down, down_block, 0)
    exchange(blocks_down - 1)

    def finish(block, carry):
        combine(block)
        return carry

    lax.fori_loop(blocks_down - lag, blocks_down, finish, 0)

    def settle_send(distance, carry):
        send_copy(distance).wait_send()
        return carry

    lax.fori_loop(1, chips, settle_send, 0)

    def settle_block(block, carry):
        give_copy(block).wait_send()

        def settle_back(distance, inner):
            back_copy(block, distance).wait_send()
            return inner

        return lax.fori_loop(1, chips, settle_back, carry)

    lax.fori_loop(0, blocks_down, settle_block, 0)


def on_device(tokens, route_ids, route_weight, gate_weight, up_weight, down_weight):
    n = lax.axis_size("hidden")
    chips = n // 2
    steps, rows, width = tokens.shape
    units = gate_weight.shape[1]
    places = steps * MOST
    half = chips * places
    blocks = width // WIDE
    down_rows = min(UNIT, units)
    total_units = 2 * (width // UNIT) * (units // WIDE) + (units // down_rows) * blocks
    slots = min(SLOTS, total_units)
    bf16, f32 = jnp.bfloat16, jnp.float32
    dma = pltpu.SemaphoreType.DMA
    mixed = pl.pallas_call(
        functools.partial(kernel, n),
        out_shape=jax.ShapeDtypeStruct((steps, rows, width), f32),
        in_specs=[
            pl.BlockSpec(memory_space=pltpu.VMEM),
            pl.BlockSpec(memory_space=pltpu.SMEM),
            pl.BlockSpec(memory_space=pltpu.SMEM),
            pl.BlockSpec(memory_space=pl.ANY),
            pl.BlockSpec(memory_space=pl.ANY),
            pl.BlockSpec(memory_space=pl.ANY),
        ],
        out_specs=pl.BlockSpec(memory_space=pltpu.VMEM),
        scratch_shapes=[
            pltpu.VMEM((EXPERTS, places, width), bf16),
            pltpu.VMEM((chips, places, width), bf16),
            pltpu.VMEM((chips, places, width), bf16),
            pltpu.VMEM((2 * half // 8, 8, width), f32),
            pltpu.VMEM((2 * half, width), bf16),
            pltpu.VMEM((slots, UNIT, WIDE), bf16),
            pltpu.VMEM((2 * half, units), bf16),
            pltpu.VMEM((blocks, half, WIDE), f32),
            pltpu.VMEM((blocks, half, WIDE), bf16),
            pltpu.VMEM((blocks, half, WIDE), bf16),
            pltpu.VMEM((blocks, chips, places, WIDE), bf16),
            pltpu.VMEM((blocks, chips, places, WIDE), bf16),
            pltpu.VMEM((steps * rows, half), f32),
            dma((slots,)),
            dma((chips,)),
            dma((chips,)),
            dma((chips,)),
            dma((chips,)),
            dma((blocks,)),
            dma((blocks,)),
            dma((blocks, chips)),
            dma((blocks, chips)),
            dma,
        ],
        compiler_params=pltpu.CompilerParams(
            collective_id=0, has_side_effects=True, vmem_limit_bytes=64 * 1024 * 1024
        ),
        cost_estimate=pl.CostEstimate(
            flops=12 * half * width * units, bytes_accessed=6 * width * units, transcendentals=0
        ),
    )(tokens, route_ids, route_weight, gate_weight, up_weight, down_weight)
    return mixed.astype(bf16)


def solution(mesh):
    placed = (
        P(None, ("parts", "hidden"), None),
        P(None, ("parts", "hidden"), None),
        P(None, ("parts", "hidden"), None),
        P(None, "hidden"),
        P(None, "hidden"),
        P("hidden", None),
    )
    return jax.shard_map(
        on_device,
        mesh=mesh,
        in_specs=placed,
        out_specs=P(None, ("parts", "hidden"), None),
        check_vma=False,
    )
```

time: 75.6 us -> 43.4 us (0.57)
  Pallas kernels: 0 us -> 38.9 us
  matrix products: 32.3 us -> 0 us
  waiting for transfers between devices: 22.8 us -> 0 us
  starting transfers between devices: 10.9 us -> 0 us
  local copies, waits for them, and re-layouts: 6.04 us -> 2.72 us
  other arithmetic: 2.98 us -> 1.53 us
    pallas_call x0 -> x1, Pallas kernels: none -> 38.9 us  [on_device(): pl.pallas_call(functools.partial(kernel, n), out_shape=jax.ShapeDtypeStru...]
    dot_general x4 -> x0, matrix products: 32.3 us -> none  [the longest x1 19.9 us: expert_apply(): jnp.dot(hidden, down_weight, preferred_element_type=jnp.float32)]
    all_to_all x2 -> x0, waiting for transfers between devices: 22.8 us -> none  [the longest x1 11.6 us: on_device(): lax.all_to_all(expert_apply(lax.all_to_all(packed, 'hidden', split_axis=0...]
    all_to_all x2 -> x0, starting transfers between devices: 10.9 us -> none  [the longest x1 7.36 us: on_device(): lax.all_to_all(packed, 'hidden', split_axis=0, concat_axis=0, tiled=True)]
    gather x8 -> x0, local copies, waits for them, and re-layouts: 2.89 us -> none  [combine(): fetched = jnp.take_along_axis(summed, slot_of[:, :, None], axis=1)]
    unnamed x0 -> x2, local copies, waits for them, and re-layouts: none -> 2.72 us
    convert_element_type x0 -> x1, other arithmetic: none -> 1.53 us  [on_device(): return mixed.astype(bf16)]
    concatenate x1 -> x0, other arithmetic: 1.15 us -> none  [on_device(): jnp.concatenate([pack_rows(tables[step_index][0], tokens[step_index], gro...]
  transfers between devices with their start and end apart: 2 -> 0, of which waited for: 2 -> 0; matrix products, arithmetic and copies ran while one was open for 2% -> 0% of each run, Pallas kernels for 0% -> 0%
where the time goes in v1:
time: 43.4 us; the launch traced here: 43.2 us
  Pallas kernels  38.9 us (90%)
  local copies, waits for them, and re-layouts  2.72 us (6%)
  other arithmetic  1.53 us (4%)
    pallas_call x1, Pallas kernels, on_device(): pl.pallas_call(functools.partial(kernel, n), out_shape=jax.ShapeDtypeStru...  38.9 us
    unnamed x2, local copies, waits for them, and re-layouts  2.72 us
    convert_element_type x1, other arithmetic, on_device(): return mixed.astype(bf16)  1.53 us

profile of v1, /device:TPU:0, one launch (start us, length us, event | category | flops | bytes accessed | tf_op | source)
XLA Modules:
  0.0 43.2 jit_solution(1896219198968003961)
XLA Ops:
  0.0 1.4 %copy.7.ids = s32[2,4,2]{2,1,0:T(4,128)} copy(s32[2,4,2]{1,2,0:T(2,128)} %param.7) | data formatting | bytes 128 | tf_op args[1]
  1.4 1.4 %copy.8.shares = f32[2,4,2]{2,1,0:T(4,128)} copy(f32[2,4,2]{1,2,0:T(2,128)} %param.8) | data formatting | bytes 128 | tf_op args[2]
  2.7 38.9 %shard_map.64 = f32[2,4,3072]{2,1,0:T(4,128)} custom-call(bf16[2,4,3072]{2,1,0:T(4,128)(2,1)} %tokens.1, s32[2,4,2]{2,1,0:T(4,128)} %copy.7.ids, f32[2,4,2]{2,1,0:T(4,128)} %copy.8.shares, bf16[3072,4096]{1,0:T(8,128)(2,1)} %gate.1, bf16[3072,4096]{1,0:T(8,128)(2,1)} %up.1, bf16[4096,3072]{1,0:T(8,128)(2,1)} %down.1), custom_call_target="tpu_custom_call" | custom-call | flops 4831838208 | bytes 75497472 | tf_op jit(solution)/shard_map/pallas_call | solution.py:408
  41.7 1.5 %convert_element_type.3 = bf16[2,4,3072]{2,1,0:T(4,128)(2,1)} convert(f32[2,4,3072]{2,1,0:T(4,128)} %shard_map.64) | non-fusion elementwise | flops 24576 | bytes 147456 | tf_op jit(solution)/shard_map/convert_element_type | solution.py:452

commit v2 on v1

--- a/solution.py
+++ b/solution.py
@@ -10,42 +10,52 @@
 EXPERTS = 8
 MOST = 2
 UNIT = 1024
-WIDE = 512
-SLOTS = 56
+WIDE = 1024
+PART = 512
+FED = 128
+SLOTS = 28
 MESH = pl.DeviceIdType.MESH
 
 
-def routing(ids, shares, steps, rows, experts, step_of, slot_of, row, owner_axis):
-    shape = experts.shape
-    before = jnp.zeros(shape, jnp.int32)
-    picked = jnp.zeros(shape, jnp.int32)
-    factor = jnp.zeros(shape, jnp.float32)
-    for number in range(steps * rows):
-        step, place = number // rows, number % rows
-        first, second = ids[step, place, 0], ids[step, place, 1]
-        named_first, named_second = experts == first, experts == second
-        named = jnp.where(named_first | named_second, 1, 0)
-        share = jnp.where(named_first, shares[step, place, 0], 0.0) + jnp.where(
-            named_second, shares[step, place, 1], 0.0
-        )
-        here = row == number
-        picked = jnp.where(here, named, picked)
-        factor = jnp.where(here, share, factor)
-        later = (row > number) & (row < (step + 1) * rows)
-        before = before + jnp.where(later, named, 0)
-    chosen = (picked == 1) & (before == slot_of) & (row // rows == step_of)
-    return jnp.where(chosen, 1.0, 0.0), jnp.where(chosen, factor, 0.0)
+def routing(ids, shares, rows, place_expert, place_step, place_slot):
+    steps = ids.shape[0]
+    shape = place_expert.shape
+
+    def along(ref, choice):
+        return jnp.concatenate([ref[step, choice : choice + 1, :] for step in range(steps)], axis=1)
+
+    named_first = along(ids, 0) == place_expert
+    named_second = along(ids, 1) == place_expert
+    picked = jnp.where(named_first | named_second, 1.0, 0.0)
+    earlier = lax.broadcasted_iota(jnp.int32, (shape[1], shape[1]), 0)
+    later = lax.broadcasted_iota(jnp.int32, (shape[1], shape[1]), 1)
+    ahead = jnp.where((earlier < later) & (earlier // rows == later // rows), 1.0, 0.0)
+    before = jnp.dot(picked, ahead, preferred_element_type=jnp.float32)
+    row = lax.broadcasted_iota(jnp.int32, shape, 1)
+    same = (row // rows == place_step) & (before == place_slot.astype(jnp.float32))
+    chosen = jnp.where(same, picked, 0.0)
+    share = jnp.where(named_first, along(shares, 0), 0.0) + jnp.where(
+        named_second, along(shares, 1), 0.0
+    )
+    return chosen, chosen * share
+
+
+def product(rows, weights):
+    return jnp.dot(rows, weights, preferred_element_type=jnp.float32)
 
 
 def kernel(
     n,
-    tokens,
-    ids,
-    shares,
+    tokens_in,
+    ids_in,
+    shares_in,
     gate,
     up,
     down,
     out,
+    tokens,
+    ids,
+    shares,
     send,
     near,
     far,
@@ -69,9 +79,11 @@
     sums_sem,
     back_sem,
     own_sem,
+    in_sem,
 ):
     steps, rows, width = tokens.shape
     units = gate.shape[1]
+    wide = min(WIDE, units)
     chips = n // 2
     places = steps * MOST
     per_expert = chips // EXPERTS
@@ -80,16 +92,21 @@
     sibling = {"hidden": chip * 2 + (1 - core)}
     slots = w.shape[0]
     deep = width // UNIT
-    blocks_up = units // WIDE
+    blocks_up = units // wide
     first_units = 2 * deep * blocks_up
     down_rows = min(UNIT, units)
     down_deep = units // down_rows
     blocks_down = width // WIDE
+    parts = WIDE // PART
     down_units = down_deep * blocks_down
     early = min(down_units, slots - first_units)
 
     def peer(distance):
-        return lax.rem(chip + distance, chips)
+        other, bit = 0, 1
+        while bit < chips:
+            other = other + bit * lax.rem(chip // bit + distance // bit, 2)
+            bit = 2 * bit
+        return other
 
     def device(other):
         return {"hidden": other * 2 + core}
@@ -97,8 +114,8 @@
     def up_copy(block, i, ref, base):
         slot = block * 2 * deep + base + i
         return pltpu.make_async_copy(
-            ref.at[pl.ds(i * UNIT, UNIT), pl.ds(pl.multiple_of(block * WIDE, WIDE), WIDE)],
-            w.at[slot],
+            ref.at[pl.ds(i * UNIT, UNIT), pl.ds(pl.multiple_of(block * wide, wide), wide)],
+            w.at[slot, :, pl.ds(0, wide)],
             w_sem.at[slot],
         )
 
@@ -125,8 +142,19 @@
         pl.semaphore_signal(barrier, inc=1, device_id=device(peer(distance)), device_id_type=MESH)
         return carry
 
-    lax.fori_loop(1, chips, greet, 0)
+    def farthest_first(step):
+        lax.fori_loop(0, chips - 1, lambda i, carry: step(chips - 1 - i, carry), 0)
+
+    farthest_first(greet)
     pl.semaphore_signal(barrier, inc=1, device_id=sibling, device_id_type=MESH)
+    inputs = [
+        pltpu.make_async_copy(source, target, in_sem.at[i])
+        for i, (source, target) in enumerate(
+            [(ids_in, ids), (shares_in, shares), (tokens_in, tokens)]
+        )
+    ]
+    for copy in inputs:
+        copy.start()
 
     def start_up(block, carry):
         for copy in up_copies(block):
@@ -135,11 +163,11 @@
 
     lax.fori_loop(0, blocks_up, start_up, 0)
 
-    many = EXPERTS * places
-    place = lax.broadcasted_iota(jnp.int32, (many, steps * rows), 0)
-    row = lax.broadcasted_iota(jnp.int32, (many, steps * rows), 1)
+    for copy in inputs:
+        copy.wait()
+    place = lax.broadcasted_iota(jnp.int32, (EXPERTS * places, steps * rows), 0)
     chooser, _ = routing(
-        ids, shares, steps, rows, place // places, place % places // MOST, place % MOST, row, 1
+        ids, shares, rows, place // places, place % places // MOST, place % MOST
     )
     owned = jnp.concatenate([tokens[step].astype(jnp.float32) for step in range(steps)], axis=0)
     packed = jnp.dot(chooser, owned, preferred_element_type=jnp.float32)
@@ -183,7 +211,7 @@
         send_copy(distance).start()
         return carry
 
-    lax.fori_loop(1, chips, start_send, 0)
+    farthest_first(start_send)
     own = pltpu.make_async_copy(send.at[chip // per_expert], near.at[chip], own_sem)
     own.start()
 
@@ -197,28 +225,23 @@
     pass_copy(chip).start()
 
     def forward(distance, carry):
-        source = lax.rem(chip - distance + chips, chips)
+        source = peer(distance)
         arrival(source).wait_recv()
         pass_copy(source).start()
         return carry
 
     lax.fori_loop(1, chips, forward, 0)
 
-    count = chips * places
-    row = lax.broadcasted_iota(jnp.int32, (steps * rows, count), 0)
-    place = lax.broadcasted_iota(jnp.int32, (steps * rows, count), 1)
+    place = lax.broadcasted_iota(jnp.int32, (chips * places, steps * rows), 0)
     _, found = routing(
         ids,
         shares,
-        steps,
         rows,
         place // (places * per_expert),
         place % places // MOST,
         place % MOST,
-        row,
-        0,
     )
-    factors[...] = found
+    factors[...] = found.T
 
     pairs = 8 // places
 
@@ -243,27 +266,22 @@
         return carry
 
     lax.fori_loop(0, chips // pairs, stage_far, 0)
-    x[...] = staged[...].reshape(x.shape).astype(jnp.bfloat16)
+    held = 2 * chips * places
+    x[pl.ds(0, held), :] = staged[...].reshape(held, width).astype(jnp.bfloat16)
+    if x.shape[0] > held:
+        x[pl.ds(held, x.shape[0] - held), :] = jnp.zeros((x.shape[0] - held, width), x.dtype)
 
     def up_block(block, carry):
         copies = up_copies(block)
         base = block * 2 * deep
         for copy in copies[:deep]:
             copy.wait()
-        gated = jnp.dot(
-            x[...],
-            w[pl.ds(base, deep)].reshape(width, WIDE),
-            preferred_element_type=jnp.float32,
-        )
+        gated = product(x[...], w[pl.ds(base, deep), :, pl.ds(0, wide)].reshape(width, wide))
         for copy in copies[deep:]:
             copy.wait()
-        upward = jnp.dot(
-            x[...],
-            w[pl.ds(base + deep, deep)].reshape(width, WIDE),
-            preferred_element_type=jnp.float32,
-        )
+        upward = product(x[...], w[pl.ds(base + deep, deep), :, pl.ds(0, wide)].reshape(width, wide))
         value = gated / (1.0 + jnp.exp(-gated)) * upward
-        hidden[:, pl.ds(pl.multiple_of(block * WIDE, WIDE), WIDE)] = value.astype(jnp.bfloat16)
+        hidden[:, pl.ds(pl.multiple_of(block * wide, wide), wide)] = value.astype(jnp.bfloat16)
         for i in range(2 * deep):
             number = early + block * 2 * deep + i
 
@@ -308,14 +326,16 @@
             device_id_type=MESH,
         )
 
-    def compute(block):
-        for i in range(down_deep):
-            down_copy(block * down_deep + i).wait()
-        slot = lax.rem(first_units + block * down_deep, slots)
-        weights = w[pl.ds(slot, down_deep), pl.ds(0, down_rows), :].reshape(units, WIDE)
-        partial = jnp.dot(hidden[...], weights, preferred_element_type=jnp.float32)
+    def compute(group, part):
+        block = group * parts + part
+        if part == 0:
+            for i in range(down_deep):
+                down_copy(group * down_deep + i).wait()
+        slot = lax.rem(first_units + group * down_deep, slots)
+        weights = w[pl.ds(slot, down_deep), pl.ds(0, down_rows), pl.ds(part * PART, PART)]
+        partial = product(hidden[...], weights.reshape(units, PART))
         kept[block] = partial[:half]
-        give[block] = partial[half:].astype(jnp.bfloat16)
+        give[block] = partial[half : 2 * half].astype(jnp.bfloat16)
         give_copy(block).start()
 
     def exchange(block):
@@ -328,12 +348,12 @@
             back_copy(block, distance).start()
             return carry
 
-        lax.fori_loop(1, chips, start_back, 0)
+        farthest_first(start_back)
         back[block, chip] = sums[block, chip]
 
     def combine(block):
         def await_back(distance, carry):
-            back_arrival(block, lax.rem(chip - distance + chips, chips)).wait_recv()
+            back_arrival(block, peer(distance)).wait_recv()
             return carry
 
         lax.fori_loop(1, chips, await_back, 0)
@@ -346,33 +366,35 @@
             preferred_element_type=jnp.float32,
             precision=lax.Precision.HIGHEST,
         )
-        columns = pl.ds(pl.multiple_of(block * WIDE, WIDE), WIDE)
+        columns = pl.ds(pl.multiple_of(block * PART, PART), PART)
         for step in range(steps):
             out[step, :, columns] = mixed[step * rows : (step + 1) * rows]
 
-    lag = 3
-
-    def down_block(block, carry):
-        compute(block)
-
-        @pl.when(block >= 1)
-        def _():
-            exchange(block - 1)
-
-        @pl.when(block >= lag)
-        def _():
-            combine(block - lag)
-
-        return carry
-
-    lax.fori_loop(0, blocks_down, down_block, 0)
-    exchange(blocks_down - 1)
+    lag = min(4, blocks_down * parts)
+
+    def down_group(group, carry):
+        for part in range(parts):
+            block = group * parts + part
+            compute(group, part)
+
+            @pl.when(block >= 1)
+            def _():
+                exchange(block - 1)
+
+            @pl.when(block >= lag)
+            def _():
+                combine(block - lag)
+
+        return carry
+
+    lax.fori_loop(0, blocks_down, down_group, 0)
+    exchange(blocks_down * parts - 1)
 
     def finish(block, carry):
         combine(block)
         return carry
 
-    lax.fori_loop(blocks_down - lag, blocks_down, finish, 0)
+    lax.fori_loop(blocks_down * parts - lag, blocks_down * parts, finish, 0)
 
     def settle_send(distance, carry):
         send_copy(distance).wait_send()
@@ -389,7 +411,7 @@
 
         return lax.fori_loop(1, chips, settle_back, carry)
 
-    lax.fori_loop(0, blocks_down, settle_block, 0)
+    lax.fori_loop(0, blocks_down * parts, settle_block, 0)
 
 
 def on_device(tokens, route_ids, route_weight, gate_weight, up_weight, down_weight):
@@ -397,11 +419,14 @@
     chips = n // 2
     steps, rows, width = tokens.shape
     units = gate_weight.shape[1]
+    choices = route_ids.shape[2]
     places = steps * MOST
     half = chips * places
-    blocks = width // WIDE
+    blocks = width // PART
     down_rows = min(UNIT, units)
-    total_units = 2 * (width // UNIT) * (units // WIDE) + (units // down_rows) * blocks
+    wide = min(WIDE, units)
+    total_units = 2 * (width // UNIT) * (units // wide) + (units // down_rows) * (width // WIDE)
+    fed = max(FED, 2 * half)
     slots = min(SLOTS, total_units)
     bf16, f32 = jnp.bfloat16, jnp.float32
     dma = pltpu.SemaphoreType.DMA
@@ -409,27 +434,30 @@
         functools.partial(kernel, n),
         out_shape=jax.ShapeDtypeStruct((steps, rows, width), f32),
         in_specs=[
-            pl.BlockSpec(memory_space=pltpu.VMEM),
-            pl.BlockSpec(memory_space=pltpu.SMEM),
-            pl.BlockSpec(memory_space=pltpu.SMEM),
+            pl.BlockSpec(memory_space=pl.ANY),
+            pl.BlockSpec(memory_space=pl.ANY),
+            pl.BlockSpec(memory_space=pl.ANY),
             pl.BlockSpec(memory_space=pl.ANY),
             pl.BlockSpec(memory_space=pl.ANY),
             pl.BlockSpec(memory_space=pl.ANY),
         ],
         out_specs=pl.BlockSpec(memory_space=pltpu.VMEM),
         scratch_shapes=[
+            pltpu.VMEM((steps, rows, width), bf16),
+            pltpu.VMEM((steps, choices, rows), jnp.int32),
+            pltpu.VMEM((steps, choices, rows), f32),
             pltpu.VMEM((EXPERTS, places, width), bf16),
             pltpu.VMEM((chips, places, width), bf16),
             pltpu.VMEM((chips, places, width), bf16),
             pltpu.VMEM((2 * half // 8, 8, width), f32),
-            pltpu.VMEM((2 * half, width), bf16),
+            pltpu.VMEM((fed, width), bf16),
             pltpu.VMEM((slots, UNIT, WIDE), bf16),
-            pltpu.VMEM((2 * half, units), bf16),
-            pltpu.VMEM((blocks, half, WIDE), f32),
-            pltpu.VMEM((blocks, half, WIDE), bf16),
-            pltpu.VMEM((blocks, half, WIDE), bf16),
-            pltpu.VMEM((blocks, chips, places, WIDE), bf16),
-            pltpu.VMEM((blocks, chips, places, WIDE), bf16),
+            pltpu.VMEM((fed, units), bf16),
+            pltpu.VMEM((blocks, half, PART), f32),
+            pltpu.VMEM((blocks, half, PART), bf16),
+            pltpu.VMEM((blocks, half, PART), bf16),
+            pltpu.VMEM((blocks, chips, places, PART), bf16),
+            pltpu.VMEM((blocks, chips, places, PART), bf16),
             pltpu.VMEM((steps * rows, half), f32),
             dma((slots,)),
             dma((chips,)),
@@ -441,6 +469,7 @@
             dma((blocks, chips)),
             dma((blocks, chips)),
             dma,
+            dma((3,)),
         ],
         compiler_params=pltpu.CompilerParams(
             collective_id=0, has_side_effects=True, vmem_limit_bytes=64 * 1024 * 1024
@@ -448,7 +477,7 @@
         cost_estimate=pl.CostEstimate(
             flops=12 * half * width * units, bytes_accessed=6 * width * units, transcendentals=0
         ),
-    )(tokens, route_ids, route_weight, gate_weight, up_weight, down_weight)
+    )(tokens, route_ids.swapaxes(1, 2), route_weight.swapaxes(1, 2), gate_weight, up_weight, down_weight)
     return mixed.astype(bf16)
 
 

time: 43.4 us -> 38.3 us (0.88)
  local copies, waits for them, and re-layouts: 2.72 us -> 0 us
  Pallas kernels: 38.9 us -> 36.6 us
    unnamed x2 -> x0, local copies, waits for them, and re-layouts: 2.72 us -> none
    pallas_call x1, Pallas kernels: 38.9 us -> 36.6 us  [on_device(): pl.pallas_call(functools.partial(kernel, n), out_shape=jax.ShapeDtypeStru...]
where the time goes in v2:
time: 38.3 us; the launch traced here: 38.2 us
  Pallas kernels  36.6 us (96%)
  other arithmetic  1.53 us (4%)
    pallas_call x1, Pallas kernels, on_device(): pl.pallas_call(functools.partial(kernel, n), out_shape=jax.ShapeDtypeStru...  36.6 us
    convert_element_type x1, other arithmetic, on_device(): return mixed.astype(bf16)  1.53 us

profile of v2, /device:TPU:0, one launch (start us, length us, event | category | flops | bytes accessed | tf_op | source)
XLA Modules:
  0.0 38.2 jit_solution(1242906898496837348)
XLA Ops:
  0.0 36.6 %shard_map.64 = f32[2,4,3072]{2,1,0:T(4,128)} custom-call(bf16[2,4,3072]{2,1,0:T(4,128)(2,1)} %tokens_in.1, s32[2,2,4]{2,1,0:T(2,128)} %bitcast.2, f32[2,2,4]{2,1,0:T(2,128)} %bitcast.3, bf16[3072,4096]{1,0:T(8,128)(2,1)} %gate.1, bf16[3072,4096]{1,0:T(8,128)(2,1)} %up.1, bf16[4096,3072]{1,0:T(8,128)(2,1)} %down.1), custom_call_target="tpu_custom_call" | custom-call | flops 4831838208 | bytes 75497472 | tf_op jit(solution)/shard_map/pallas_call | solution.py:433
  36.7 1.5 %convert_element_type.3 = bf16[2,4,3072]{2,1,0:T(4,128)(2,1)} convert(f32[2,4,3072]{2,1,0:T(4,128)} %shard_map.64) | non-fusion elementwise | flops 24576 | bytes 147456 | tf_op jit(solution)/shard_map/convert_element_type | solution.py:481

commit v3 on v2

--- a/solution.py
+++ b/solution.py
@@ -99,7 +99,7 @@
     blocks_down = width // WIDE
     parts = WIDE // PART
     down_units = down_deep * blocks_down
-    early = min(down_units, slots - first_units)
+    early = min(down_units, slots - first_units) // down_deep
 
     def peer(distance):
         other, bit = 0, 1
@@ -116,7 +116,7 @@
         return pltpu.make_async_copy(
             ref.at[pl.ds(i * UNIT, UNIT), pl.ds(pl.multiple_of(block * wide, wide), wide)],
             w.at[slot, :, pl.ds(0, wide)],
-            w_sem.at[slot],
+            w_sem.at[slot, 0],
         )
 
     def up_copies(block):
@@ -124,17 +124,22 @@
             up_copy(block, i, up, deep) for i in range(deep)
         ]
 
-    def down_copy(number):
-        block, i = number // down_deep, lax.rem(number, down_deep)
+    def down_copy(number, part):
+        group, i = number // down_deep, lax.rem(number, down_deep)
         slot = lax.rem(first_units + number, slots)
         return pltpu.make_async_copy(
             down.at[
                 pl.ds(pl.multiple_of(i * down_rows, down_rows), down_rows),
-                pl.ds(pl.multiple_of(block * WIDE, WIDE), WIDE),
+                pl.ds(pl.multiple_of(group * WIDE + part * PART, PART), PART),
             ],
-            w.at[slot, pl.ds(0, down_rows), :],
-            w_sem.at[slot],
-        )
+            w.at[slot, pl.ds(0, down_rows), pl.ds(part * PART, PART)],
+            w_sem.at[slot, part],
+        )
+
+    def start_group(group):
+        for part in range(parts):
+            for i in range(down_deep):
+                down_copy(group * down_deep + i, part).start()
 
     barrier = pltpu.get_barrier_semaphore()
 
@@ -174,6 +179,10 @@
     for expert in range(EXPERTS):
         send[expert] = packed[expert * places : (expert + 1) * places].astype(jnp.bfloat16)
 
+    held = 2 * chips * places
+    if x.shape[0] > held:
+        x[pl.ds(held, x.shape[0] - held), :] = jnp.zeros((x.shape[0] - held, width), x.dtype)
+
     pl.semaphore_wait(barrier, chips)
 
     def send_copy(distance):
@@ -215,8 +224,8 @@
     own = pltpu.make_async_copy(send.at[chip // per_expert], near.at[chip], own_sem)
     own.start()
 
-    def start_down(number, carry):
-        down_copy(number).start()
+    def start_down(group, carry):
+        start_group(group)
         return carry
 
     lax.fori_loop(0, early, start_down, 0)
@@ -266,28 +275,24 @@
         return carry
 
     lax.fori_loop(0, chips // pairs, stage_far, 0)
-    held = 2 * chips * places
     x[pl.ds(0, held), :] = staged[...].reshape(held, width).astype(jnp.bfloat16)
-    if x.shape[0] > held:
-        x[pl.ds(held, x.shape[0] - held), :] = jnp.zeros((x.shape[0] - held, width), x.dtype)
 
     def up_block(block, carry):
         copies = up_copies(block)
         base = block * 2 * deep
-        for copy in copies[:deep]:
+        for copy in copies:
             copy.wait()
         gated = product(x[...], w[pl.ds(base, deep), :, pl.ds(0, wide)].reshape(width, wide))
-        for copy in copies[deep:]:
-            copy.wait()
         upward = product(x[...], w[pl.ds(base + deep, deep), :, pl.ds(0, wide)].reshape(width, wide))
         value = gated / (1.0 + jnp.exp(-gated)) * upward
         hidden[:, pl.ds(pl.multiple_of(block * wide, wide), wide)] = value.astype(jnp.bfloat16)
-        for i in range(2 * deep):
-            number = early + block * 2 * deep + i
-
-            @pl.when(number < down_units)
+        first = block * 2 * deep // down_deep
+        last = (block + 1) * 2 * deep // down_deep
+        for i in range(-(-2 * deep // down_deep)):
+
+            @pl.when((first + i < last) & (early + first + i < blocks_down))
             def _():
-                down_copy(number).start()
+                start_group(early + first + i)
 
         return carry
 
@@ -328,9 +333,8 @@
 
     def compute(group, part):
         block = group * parts + part
-        if part == 0:
-            for i in range(down_deep):
-                down_copy(group * down_deep + i).wait()
+        for i in range(down_deep):
+            down_copy(group * down_deep + i, part).wait()
         slot = lax.rem(first_units + group * down_deep, slots)
         weights = w[pl.ds(slot, down_deep), pl.ds(0, down_rows), pl.ds(part * PART, PART)]
         partial = product(hidden[...], weights.reshape(units, PART))
@@ -388,13 +392,8 @@
         return carry
 
     lax.fori_loop(0, blocks_down, down_group, 0)
-    exchange(blocks_down * parts - 1)
-
-    def finish(block, carry):
-        combine(block)
-        return carry
-
-    lax.fori_loop(blocks_down * parts - lag, blocks_down * parts, finish, 0)
+    final = blocks_down * parts - 1
+    exchange(final)
 
     def settle_send(distance, carry):
         send_copy(distance).wait_send()
@@ -411,7 +410,15 @@
 
         return lax.fori_loop(1, chips, settle_back, carry)
 
-    lax.fori_loop(0, blocks_down * parts, settle_block, 0)
+    lax.fori_loop(0, final, settle_block, 0)
+
+    def finish(block, carry):
+        combine(block)
+        return carry
+
+    lax.fori_loop(final + 1 - lag, final, finish, 0)
+    settle_block(final, 0)
+    combine(final)
 
 
 def on_device(tokens, route_ids, route_weight, gate_weight, up_weight, down_weight):
@@ -432,7 +439,7 @@
     dma = pltpu.SemaphoreType.DMA
     mixed = pl.pallas_call(
         functools.partial(kernel, n),
-        out_shape=jax.ShapeDtypeStruct((steps, rows, width), f32),
+        out_shape=pltpu.VMEM((steps, rows, width), f32),
         in_specs=[
             pl.BlockSpec(memory_space=pl.ANY),
             pl.BlockSpec(memory_space=pl.ANY),
@@ -459,7 +466,7 @@
             pltpu.VMEM((blocks, chips, places, PART), bf16),
             pltpu.VMEM((blocks, chips, places, PART), bf16),
             pltpu.VMEM((steps * rows, half), f32),
-            dma((slots,)),
+            dma((slots, WIDE // PART)),
             dma((chips,)),
             dma((chips,)),
             dma((chips,)),
@@ -472,7 +479,7 @@
             dma((3,)),
         ],
         compiler_params=pltpu.CompilerParams(
-            collective_id=0, has_side_effects=True, vmem_limit_bytes=64 * 1024 * 1024
+            collective_id=0, has_side_effects=True, vmem_limit_bytes=66_600_000
         ),
         cost_estimate=pl.CostEstimate(
             flops=12 * half * width * units, bytes_accessed=6 * width * units, transcendentals=0

time: 38.3 us -> 35 us (0.914)
  Pallas kernels: 36.6 us -> 34.2 us
  other arithmetic: 1.53 us -> 0.64 us
    pallas_call x1, Pallas kernels: 36.6 us -> 34.2 us  [on_device(): pl.pallas_call(functools.partial(kernel, n), out_shape=pltpu.VMEM((steps,...]
    convert_element_type x1, other arithmetic: 1.53 us -> 0.64 us  [on_device(): return mixed.astype(bf16)]
where the time goes in v3:
time: 35 us; the launch traced here: 34.9 us
  Pallas kernels  34.2 us (98%)
  other arithmetic  0.64 us (2%)
    pallas_call x1, Pallas kernels, on_device(): pl.pallas_call(functools.partial(kernel, n), out_shape=pltpu.VMEM((steps,...  34.2 us

profile of v3, /device:TPU:0, one launch (start us, length us, event | category | flops | bytes accessed | tf_op | source)
XLA Modules:
  0.0 34.9 jit_solution(11602468163209249443)
XLA Ops:
  0.0 34.2 %shard_map.64 = f32[2,4,3072]{2,1,0:T(4,128)S(1)} custom-call(bf16[2,4,3072]{2,1,0:T(4,128)(2,1)} %tokens_in.1, s32[2,2,4]{2,1,0:T(2,128)} %bitcast.2, f32[2,2,4]{2,1,0:T(2,128)} %bitcast.3, bf16[3072,4096]{1,0:T(8,128)(2,1)} %gate.1, bf16[3072,4096]{1,0:T(8,128)(2,1)} %up.1, bf16[4096,3072]{1,0:T(8,128)(2,1)} %down.1), custom_call_target="tpu_custom_call" | custom-call | flops 4831838208 | bytes 75497472 | tf_op jit(solution)/shard_map/pallas_call | solution.py:440
  34.2 0.6 %convert_element_type.3 = bf16[2,4,3072]{2,1,0:T(4,128)(2,1)} convert(f32[2,4,3072]{2,1,0:T(4,128)S(1)} %shard_map.64) | non-fusion elementwise | flops 24576 | bytes 147456 | tf_op jit(solution)/shard_map/convert_element_type | solution.py:488

commit v4 on v3

--- a/solution.py
+++ b/solution.py
@@ -182,6 +182,7 @@
     held = 2 * chips * places
     if x.shape[0] > held:
         x[pl.ds(held, x.shape[0] - held), :] = jnp.zeros((x.shape[0] - held, width), x.dtype)
+        hidden[pl.ds(held, x.shape[0] - held), :] = jnp.zeros((x.shape[0] - held, units), x.dtype)
 
     pl.semaphore_wait(barrier, chips)
 
@@ -284,8 +285,9 @@
             copy.wait()
         gated = product(x[...], w[pl.ds(base, deep), :, pl.ds(0, wide)].reshape(width, wide))
         upward = product(x[...], w[pl.ds(base + deep, deep), :, pl.ds(0, wide)].reshape(width, wide))
+        gated, upward = gated[:held], upward[:held]
         value = gated / (1.0 + jnp.exp(-gated)) * upward
-        hidden[:, pl.ds(pl.multiple_of(block * wide, wide), wide)] = value.astype(jnp.bfloat16)
+        hidden[pl.ds(0, held), pl.ds(pl.multiple_of(block * wide, wide), wide)] = value.astype(jnp.bfloat16)
         first = block * 2 * deep // down_deep
         last = (block + 1) * 2 * deep // down_deep
         for i in range(-(-2 * deep // down_deep)):

time: 35 us -> 35 us (level)
  no operation moved by 1% of the time
where the time goes in v4:
time: 35 us; the launch traced here: 34.8 us
  Pallas kernels  34.2 us (98%)
  other arithmetic  0.64 us (2%)
    pallas_call x1, Pallas kernels, on_device(): pl.pallas_call(functools.partial(kernel, n), out_shape=pltpu.VMEM((steps,...  34.2 us

profile of v4, /device:TPU:0, one launch (start us, length us, event | category | flops | bytes accessed | tf_op | source)
XLA Modules:
  0.0 34.8 jit_solution(9496151059402625815)
XLA Ops:
  0.0 34.2 %shard_map.64 = f32[2,4,3072]{2,1,0:T(4,128)S(1)} custom-call(bf16[2,4,3072]{2,1,0:T(4,128)(2,1)} %tokens_in.1, s32[2,2,4]{2,1,0:T(2,128)} %bitcast.2, f32[2,2,4]{2,1,0:T(2,128)} %bitcast.3, bf16[3072,4096]{1,0:T(8,128)(2,1)} %gate.1, bf16[3072,4096]{1,0:T(8,128)(2,1)} %up.1, bf16[4096,3072]{1,0:T(8,128)(2,1)} %down.1), custom_call_target="tpu_custom_call" | custom-call | flops 4831838208 | bytes 75497472 | tf_op jit(solution)/shard_map/pallas_call | solution.py:442
  34.2 0.6 %convert_element_type.3 = bf16[2,4,3072]{2,1,0:T(4,128)(2,1)} convert(f32[2,4,3072]{2,1,0:T(4,128)S(1)} %shard_map.64) | non-fusion elementwise | flops 24576 | bytes 147456 | tf_op jit(solution)/shard_map/convert_element_type | solution.py:490
